TPU v7x, 32 devices: a whole 2x2x4 slice. The times are simulated.
32 devices in a mesh: groups: 2 (over y), facet: 4 (over z), subband: 4 (over x, core).
Axes of the slice: x: 2, y: 2, z: 4, core: 2. Of those that a mesh axis runs over, the one named last changes fastest.
Arguments:
- model: bfloat16 [8192, 2048], P(('groups', 'facet')), parts along dimension 0, may hold values from -6 to 6
- kernel: bfloat16 [2048, 128], P('subband'), may hold values from -0.125 to 0.125
- spectrum: float32 [8, 128], P(('groups', 'subband')), parts along dimension 0, may hold values from 0.5 to 2
- observed: bfloat16 [8, 16, 512, 128], P(('groups', 'subband'), 'facet'), parts along dimension 0, may hold values from -6 to 6
- subgrid_ids: int32 [8, 512], P('groups'), parts along dimension 0, may hold values from 0 to 4095
- owners: int32 [8], P('groups'), parts along dimension 0, may hold values from 0 to 3
Outputs:
- residual: bfloat16 [8, 2048, 128], P(('groups', 'subband')), parts along dimension 0
- dirty: bfloat16 [8192, 2048], P(('groups', 'facet', 'subband')), parts along dimension 0
There are 2 independent parts, one for each index of `groups`. A program takes and returns all parts, laid end to end along the dimension named above; an argument that names none is the same for every part. Nothing has to cross between parts.
All inputs are finite; a program needn't handle non-finite values.
Results may differ from a plain program's by a relative error of at most 0.0095.
Values may be sent and summed in bfloat16 or wider, within the bound.
A program may use at most 64 MiB of HBM per device.

v0:
```python
import jax
import jax.numpy as jnp
from jax import lax
from jax.sharding import PartitionSpec as P


def broadcast(block, axis, holder):
    block = jnp.where(lax.axis_index(axis) == holder, block, jnp.zeros_like(block))
    return lax.psum(block, axis)


def local(model, kernel, spectrum, observed, subgrid_ids, owners):
    full_kernel = lax.all_gather(kernel, "subband", axis=0, tiled=True)
    predicted = jnp.dot(model, full_kernel, preferred_element_type=jnp.float32).astype(jnp.bfloat16)
    spec_row = spectrum[0]
    facet_index = lax.axis_index("facet")
    sub_count = model.shape[0]
    width = predicted.shape[1]
    offset = facet_index * sub_count
    columns = lax.iota(jnp.int32, sub_count)
    span_count = subgrid_ids.shape[0]
    local_spans = observed[0]

    def step(grid_acc, span):
        local_ids = lax.dynamic_index_in_dim(subgrid_ids, span, 0, keepdims=False) - offset
        selector = (local_ids[:, None] == columns[None, :]).astype(jnp.bfloat16)
        partial_rows = jnp.dot(selector, predicted, preferred_element_type=jnp.float32) * spec_row
        owner = lax.dynamic_index_in_dim(owners, span, 0, keepdims=False)
        local_obs = lax.dynamic_index_in_dim(local_spans, span, 0, keepdims=False)
        arrived = broadcast(local_obs, "facet", owner)
        summed = lax.psum(partial_rows, "facet")
        residual_vis = arrived.astype(jnp.float32) - summed
        rounded = residual_vis.astype(jnp.bfloat16)
        grid_acc = grid_acc + lax.dot_general(
            selector, rounded, (((0,), (0,)), ((), ())), preferred_element_type=jnp.float32
        )
        return (grid_acc, rounded)

    start = jnp.zeros((sub_count, width), jnp.float32)
    grid_acc, rounded_all = lax.scan(step, start, jnp.arange(span_count, dtype=jnp.int32))
    residual = rounded_all.reshape(1, -1, width)
    weighted = (grid_acc * spec_row).astype(jnp.bfloat16)
    summed_grids = lax.psum_scatter(
        weighted.astype(jnp.float32).astype(jnp.bfloat16),
        "subband",
        scatter_dimension=0,
        tiled=True,
    ).astype(jnp.float32)
    dirty = lax.dot_general(
        summed_grids,
        full_kernel.astype(jnp.float32),
        (((1,), (1,)), ((), ())),
        precision=lax.Precision.HIGHEST,
        preferred_element_type=jnp.float32,
    )
    return (residual, dirty.astype(jnp.bfloat16))


def solution(mesh):
    return jax.shard_map(
        local,
        mesh=mesh,
        in_specs=(
            P(("groups", "facet"), None),
            P("subband", None),
            P(("groups", "subband"), None),
            P(("groups", "subband"), "facet", None, None),
            P("groups", None),
            P("groups"),
        ),
        out_specs=(P(("groups", "subband"), None, None), P(("groups", "facet", "subband"), None)),
        check_vma=False,
    )
```

profile of v0, /device:TPU:1, one launch (start us, length us, event | category | flops | bytes accessed | tf_op | source)
XLA Modules:
  0.0 378.4 jit_solution(6414523707963488975)
XLA Ops:
  8.0 8.7 %all_gather.3 = bf16[2048,128]{1,0:T(8,128)(2,1)S(1)} all-gather(bf16[512,128]{1,0:T(8,128)(2,1)} %param.9), channel_id=1, replica_groups=mesh['groups'=2,'facet'=4,'subband'=4] {'subband'}, dimensions={0}, use_global_device_ids=true | all-gather | bytes 655360 | tf_op jit(solution)/shard_map/all_gather | solution.py:13
  16.7 0.0 copy-start
  16.8 0.0 copy-start.1
  16.8 3.5 convolution_convert_fusion.1
  20.2 0.0 copy-done
  20.2 0.0 copy-done.1
  20.2 324.0 %while.13 = (s32[]{:T(128)}, f32[1024,128]{1,0:T(8,128)S(1)}, bf16[4,512,128]{2,1,0:T(8,128)(2,1)}, s32[4]{0:T(128)S(1)}, s32[4,512]{1,0:T(4,128)}, /*index=5*/s...) while((s32[]{:T(128)}, f32[1024,128]{1,0:T(8,128)S(1)}, ...), condition=%wide.region_3.4_spmd.clone, body=%wide.region_0.3_spmd.clone.sunk | while | flops 270402048 | bytes 5120867 | solution.py:40
  20.3 0.0 all-reduce.5.cloned.1.call-start
  20.3 0.6 dynamic_slice.28
  22.8 0.6 dynamic_slice.29
  24.1 1.6 select_bitcast_fusion.2
  25.7 0.0 all-reduce.5.cloned.1.call-update
  25.7 0.0 all-reduce.3.cloned.1.call-start
  25.7 0.7 dynamic-slice_subtract_fusion.2
  26.4 1.2 fusion.17
  27.7 0.0 all-reduce.3.cloned.1.call-update
  27.7 30.9 %all-reduce.5.cloned.1.call-done = bf16[512,128]{1,0:T(8,128)(2,1)} async-done(((bf16[512,128]{1,0:T(8,128)(2,1)}), bf16[512,128]{1,0:T(8,128)(2,1)}) %all-reduce.5.cloned.1.call-update) | async-done | bytes 131088 | tf_op jit(solution)/shard_map/while/body/eval_jaxpr/psum | solution.py:9
  58.5 38.6 %all-reduce.3.cloned.1.call-done = f32[512,128]{1,0:T(8,128)} async-done(((f32[512,128]{1,0:T(8,128)}), f32[512,128]{1,0:T(8,128)}) %all-reduce.3.cloned.1.call-update) | async-done | bytes 262160 | tf_op jit(solution)/shard_map/while/body/eval_jaxpr/psum | solution.py:31
  97.2 1.7 bitcast_dynamic-update-slice_fusion.2
  98.8 1.9 fusion.18
  100.8 0.0 all-reduce.5.cloned.1.call-start
  100.9 0.6 dynamic_slice.28
  103.4 0.6 dynamic_slice.29
  104.6 1.6 select_bitcast_fusion.2
  106.2 0.0 all-reduce.5.cloned.1.call-update
  106.2 0.0 all-reduce.3.cloned.1.call-start
  106.3 0.7 dynamic-slice_subtract_fusion.2
  107.0 1.2 fusion.17
  108.2 0.0 all-reduce.3.cloned.1.call-update
  108.2 31.6 %all-reduce.5.cloned.1.call-done = bf16[512,128]{1,0:T(8,128)(2,1)} async-done(((bf16[512,128]{1,0:T(8,128)(2,1)}), bf16[512,128]{1,0:T(8,128)(2,1)}) %all-reduce.5.cloned.1.call-update) | async-done | bytes 131088 | tf_op jit(solution)/shard_map/while/body/eval_jaxpr/psum | solution.py:9
  139.8 38.5 %all-reduce.3.cloned.1.call-done = f32[512,128]{1,0:T(8,128)} async-done(((f32[512,128]{1,0:T(8,128)}), f32[512,128]{1,0:T(8,128)}) %all-reduce.3.cloned.1.call-update) | async-done | bytes 262160 | tf_op jit(solution)/shard_map/while/body/eval_jaxpr/psum | solution.py:31
  178.3 1.7 bitcast_dynamic-update-slice_fusion.2
  179.9 1.9 fusion.18
  181.9 0.0 all-reduce.5.cloned.1.call-start
  182.0 0.6 dynamic_slice.28
  184.5 0.6 dynamic_slice.29
  185.7 1.6 select_bitcast_fusion.2
  187.3 0.0 all-reduce.5.cloned.1.call-update
  187.3 0.0 all-reduce.3.cloned.1.call-start
  187.4 0.7 dynamic-slice_subtract_fusion.2
  188.1 1.2 fusion.17
  189.3 0.0 all-reduce.3.cloned.1.call-update
  189.3 31.6 %all-reduce.5.cloned.1.call-done = bf16[512,128]{1,0:T(8,128)(2,1)} async-done(((bf16[512,128]{1,0:T(8,128)(2,1)}), bf16[512,128]{1,0:T(8,128)(2,1)}) %all-reduce.5.cloned.1.call-update) | async-done | bytes 131088 | tf_op jit(solution)/shard_map/while/body/eval_jaxpr/psum | solution.py:9
  220.9 38.5 %all-reduce.3.cloned.1.call-done = f32[512,128]{1,0:T(8,128)} async-done(((f32[512,128]{1,0:T(8,128)}), f32[512,128]{1,0:T(8,128)}) %all-reduce.3.cloned.1.call-update) | async-done | bytes 262160 | tf_op jit(solution)/shard_map/while/body/eval_jaxpr/psum | solution.py:31
  259.4 1.7 bitcast_dynamic-update-slice_fusion.2
  261.1 1.9 fusion.18
  263.0 0.0 all-reduce.5.cloned.1.call-start
  263.1 0.6 dynamic_slice.28
  265.6 0.6 dynamic_slice.29
  266.8 1.6 select_bitcast_fusion.2
  268.4 0.0 all-reduce.5.cloned.1.call-update
  268.4 0.0 all-reduce.3.cloned.1.call-start
  268.5 0.7 dynamic-slice_subtract_fusion.2
  269.2 1.2 fusion.17
  270.4 0.0 all-reduce.3.cloned.1.call-update
  270.4 31.6 %all-reduce.5.cloned.1.call-done = bf16[512,128]{1,0:T(8,128)(2,1)} async-done(((bf16[512,128]{1,0:T(8,128)(2,1)}), bf16[512,128]{1,0:T(8,128)(2,1)}) %all-reduce.5.cloned.1.call-update) | async-done | bytes 131088 | tf_op jit(solution)/shard_map/while/body/eval_jaxpr/psum | solution.py:9
  302.0 38.6 %all-reduce.3.cloned.1.call-done = f32[512,128]{1,0:T(8,128)} async-done(((f32[512,128]{1,0:T(8,128)}), f32[512,128]{1,0:T(8,128)}) %all-reduce.3.cloned.1.call-update) | async-done | bytes 262160 | tf_op jit(solution)/shard_map/while/body/eval_jaxpr/psum | solution.py:31
  340.7 1.7 bitcast_dynamic-update-slice_fusion.2
  342.3 1.9 fusion.18
  344.3 0.0 reduce-scatter.2.cloned.1.call-start
  344.4 0.7 multiply_convert_fusion
  345.1 0.0 reduce-scatter.2.cloned.1.call-update
  345.1 23.6 %reduce-scatter.2.cloned.1.call-done = bf16[256,128]{1,0:T(8,128)(2,1)} async-done(((bf16[1024,128]{1,0:T(8,128)(2,1)}), bf16[256,128]{1,0:T(8,128)(2,1)}) %reduce-scatter.2.cloned.1.call-update) | async-done | bytes 65552 | tf_op jit(solution)/shard_map/reduce_scatter | solution.py:43
  368.7 2.2 convolution_convert_fusion
  (3 shorter events, 0.0 us)
Async XLA Ops:
  16.7 3.5 copy-start
  16.8 3.5 copy-start.1
  20.3 38.3 %all-reduce.5.cloned.1.call-start = ((), (), s32[]{:S(2)}) async-start(), calls=%async_computation.3 | async-start | bytes 262144 | tf_op jit(solution)/shard_map/while/body/eval_jaxpr/psum | solution.py:9
  25.7 71.5 %all-reduce.3.cloned.1.call-start = ((), (), s32[]{:S(2)}) async-start(), calls=%async_computation.2 | async-start | bytes 524288 | tf_op jit(solution)/shard_map/while/body/eval_jaxpr/psum | solution.py:31
  100.8 39.0 %all-reduce.5.cloned.1.call-start = ((), (), s32[]{:S(2)}) async-start(), calls=%async_computation.3 | async-start | bytes 262144 | tf_op jit(solution)/shard_map/while/body/eval_jaxpr/psum | solution.py:9
  106.2 72.1 %all-reduce.3.cloned.1.call-start = ((), (), s32[]{:S(2)}) async-start(), calls=%async_computation.2 | async-start | bytes 524288 | tf_op jit(solution)/shard_map/while/body/eval_jaxpr/psum | solution.py:31
  181.9 39.0 %all-reduce.5.cloned.1.call-start = ((), (), s32[]{:S(2)}) async-start(), calls=%async_computation.3 | async-start | bytes 262144 | tf_op jit(solution)/shard_map/while/body/eval_jaxpr/psum | solution.py:9
  187.3 72.1 %all-reduce.3.cloned.1.call-start = ((), (), s32[]{:S(2)}) async-start(), calls=%async_computation.2 | async-start | bytes 524288 | tf_op jit(solution)/shard_map/while/body/eval_jaxpr/psum | solution.py:31
  263.0 39.0 %all-reduce.5.cloned.1.call-start = ((), (), s32[]{:S(2)}) async-start(), calls=%async_computation.3 | async-start | bytes 262144 | tf_op jit(solution)/shard_map/while/body/eval_jaxpr/psum | solution.py:9
  268.4 72.2 %all-reduce.3.cloned.1.call-start = ((), (), s32[]{:S(2)}) async-start(), calls=%async_computation.2 | async-start | bytes 524288 | tf_op jit(solution)/shard_map/while/body/eval_jaxpr/psum | solution.py:31
  344.3 24.4 %reduce-scatter.2.cloned.1.call-start = ((), (), s32[]{:S(2)}) async-start(), calls=%async_computation.1 | async-start | bytes 327680 | tf_op jit(solution)/shard_map/reduce_scatter | solution.py:43
Sparse Core Ops, SparseCore 0:
  25.8 32.6 all-reduce.4
  61.4 35.6 all-reduce.2
  106.3 33.4 all-reduce.4
  142.6 35.6 all-reduce.2
  187.5 33.4 all-reduce.4
  223.7 35.6 all-reduce.2
  268.6 33.4 all-reduce.4
  304.9 35.6 all-reduce.2
Sparse Core Ops, SparseCore 1:
  347.8 20.9 reduce-scatter.1
where the time goes:
time: 380 us; the launch traced here: 378 us
  waiting for transfers between devices  304 us (80%)
  matrix products  18.3 us (5%)
  other arithmetic  16.5 us (4%)
  between operations  15.5 us (4%)
  loops' own time  10.7 us (3%)
  blocking collectives  8.73 us (2%)
  local copies, waits for them, and re-layouts  4.71 us (1%)
    psum x4, waiting for transfers between devices, step(): summed = lax.psum(partial_rows, 'facet')  154 us
    psum x4, waiting for transfers between devices, broadcast(): return lax.psum(block, axis)  126 us
    reduce_scatter x1, waiting for transfers between devices, local(): lax.psum_scatter(weighted.astype(jnp.float32).astype(jnp.bfloat16), 'subb...  23.6 us
    another operation x1, loops' own time, local(): lax.scan(step, start, jnp.arange(span_count, dtype=jnp.int32))  10.7 us
    all_gather x1, blocking collectives, local(): full_kernel = lax.all_gather(kernel, 'subband', axis=0, tiled=True)  8.73 us
    dot_general x4, matrix products, step(): lax.dot_general(selector, rounded, (((0,), (0,)), ((), ())), preferred_el...  7.77 us
  transfers between devices with their start and end apart: 9, of which 9 were waited for; matrix products, arithmetic and copies ran while one was open for 2% of the time, Pallas kernels for 0%

commit v1 on v0

v1 whole, which is shorter than its diff:
```python
import functools

import jax
import jax.numpy as jnp
from jax import lax
from jax.experimental import pallas as pl
from jax.experimental.pallas import tpu as pltpu
from jax.sharding import PartitionSpec as P

MESH = pl.DeviceIdType.MESH
F32 = jnp.float32
BF16 = jnp.bfloat16
CHUNK = 256
LAG = 1


def remote(src, dst, send, recv, axis, target):
    return pltpu.make_async_remote_copy(
        src_ref=src, dst_ref=dst, send_sem=send, recv_sem=recv,
        device_id={axis: target}, device_id_type=MESH,
    )


def body(nf, ns, model, kernel, spectrum, observed, ids, owners, residual, dirty,
         model_v, kern, acc, pred, vals, r_in, l_in, r_out, l_out, res, grid, wsend, wrecv, dout,
         msem, ks, kr, rs, rr, ls, lr, ws, wr, osem, dsem):
    z = lax.axis_index("facet")
    s = lax.axis_index("subband")
    nx = ns // 2
    mate = s + 1 - 2 * (s % 2)
    subs, depth = model_v.shape[1], model_v.shape[2]
    spans, nblk = ids.shape
    per = nblk // CHUNK
    chunks = spans * per
    width = kernel.shape[1]

    order = [s, mate]
    for d in range(1, nx):
        order += [(s + ns - 2 * d) % ns, (mate + ns - 2 * d) % ns]
    loads = []
    for n, k in enumerate(order):
        at = pl.multiple_of(k * depth, depth)
        loads.append(pltpu.make_async_copy(model.at[:, pl.ds(at, depth)], model_v.at[n], msem.at[n]))
        loads[-1].start()

    barrier = pltpu.get_barrier_semaphore()
    for d in range(1, ns):
        pl.semaphore_signal(barrier, inc=1, device_id={"subband": (s + d) % ns}, device_id_type=MESH)

    @pl.when(z > 0)
    def _():
        pl.semaphore_signal(barrier, inc=1, device_id={"facet": z - 1}, device_id_type=MESH)

    @pl.when(z < nf - 1)
    def _():
        pl.semaphore_signal(barrier, inc=1, device_id={"facet": z + 1}, device_id_type=MESH)

    has_left = jnp.where(z > 0, 1, 0)
    has_right = jnp.where(z < nf - 1, 1, 0)
    pl.semaphore_wait(barrier, ns - 1 + has_left + has_right)

    cross = []
    for d in range(1, nx):
        c = remote(kernel, kern.at[s], ks.at[d], kr.at[d], "subband", (s + 2 * d) % ns)
        c.start()
        cross.append(c)
    near = remote(kernel, kern.at[s], ks.at[0], kr.at[0], "subband", mate)
    near.start()
    kern[s] = kernel[...]

    def add(n, k):
        loads[n].wait()
        part = jnp.dot(model_v[n], kern[k], preferred_element_type=F32)
        acc[...] = part if n == 0 else acc[...] + part

    add(0, s)
    near.wait_recv()
    add(1, mate)
    passed = []
    for d in range(1, nx):
        src = (s + ns - 2 * d) % ns
        cross[d - 1].wait_recv()
        c = remote(kern.at[src], kern.at[src], ks.at[nx + d - 1], kr.at[nx + d - 1], "subband", mate)
        c.start()
        passed.append(c)
        add(2 * d, src)
    for d in range(1, nx):
        passed[d - 1].wait_recv()
        add(2 * d + 1, (mate + ns - 2 * d) % ns)
    pred[...] = acc[...].astype(BF16)

    spec = spectrum[...]
    offset = z * subs
    grid[...] = jnp.zeros_like(grid)

    def right(i):
        return remote(r_out.at[i], r_in.at[i], rs.at[i], rr.at[i], "facet", z + 1)

    def left(i):
        return remote(l_out.at[i], l_in.at[i], ls.at[i], lr.at[i], "facet", z - 1)

    def out(i):
        at = pl.multiple_of(i * CHUNK, CHUNK)
        return pltpu.make_async_copy(res.at[i], residual.at[0, pl.ds(at, CHUNK)], osem.at[i])

    def step(t, _):
        @pl.when(t < chunks)
        def _():
            span = t // per
            row = ids[pl.ds(span, 1), pl.ds(pl.multiple_of((t % per) * CHUNK, CHUNK), CHUNK)] - offset
            column = jnp.broadcast_to(row, (128, CHUNK)).T
            lanes = lax.broadcasted_iota(jnp.int32, (CHUNK, 128), 1)
            pick = jnp.concatenate(
                [(column == lanes + 128 * j).astype(F32).astype(BF16) for j in range(subs // 128)], axis=1
            )
            rows = jnp.dot(pick, pred[...], preferred_element_type=F32)
            mine = jnp.where(owners[span] == z, 1.0, 0.0).astype(F32)
            seen = observed[0, span, pl.ds(pl.multiple_of((t % per) * CHUNK, CHUNK), CHUNK), :]
            vals[t] = seen.astype(F32) * mine - rows * spec

        i = t - LAG * z
        @pl.when(jnp.logical_and(i >= 0, i < chunks))
        def _():
            @pl.when(z == 0)
            def _():
                r_out[i] = vals[i].astype(BF16)

            @pl.when(z > 0)
            def _():
                right(i).wait_recv()
                r_out[i] = (vals[i] + r_in[i].astype(F32)).astype(BF16)

            @pl.when(z < nf - 1)
            def _():
                right(i).start()

        j = t - LAG * (nf - 1 - z)
        @pl.when(jnp.logical_and(j >= 0, j < chunks))
        def _():
            @pl.when(z == nf - 1)
            def _():
                l_out[j] = vals[j].astype(BF16)

            @pl.when(z < nf - 1)
            def _():
                left(j).wait_recv()
                l_out[j] = (vals[j] + l_in[j].astype(F32)).astype(BF16)

            @pl.when(z > 0)
            def _():
                left(j).start()

        e = t - LAG * jnp.maximum(z, nf - 1 - z)
        @pl.when(jnp.logical_and(e >= 0, e < chunks))
        def _():
            @pl.when(z == 0)
            def _():
                res[e] = l_out[e]

            @pl.when(z == nf - 1)
            def _():
                res[e] = r_out[e]

            @pl.when(jnp.logical_and(z > 0, z < nf - 1))
            def _():
                res[e] = (vals[e] + (r_in[e].astype(F32) + l_in[e].astype(F32))).astype(BF16)

            out(e).start()
            row = ids[pl.ds(e // per, 1), pl.ds(pl.multiple_of((e % per) * CHUNK, CHUNK), CHUNK)] - offset
            place = (lax.broadcasted_iota(jnp.int32, (subs, CHUNK), 0) == row).astype(F32).astype(BF16)
            grid[...] += jnp.dot(place, res[e], preferred_element_type=F32)

        return 0

    lax.fori_loop(0, chunks + LAG * (nf - 1), step, 0)

    share = subs // ns
    wsend[...] = (grid[...] * spec).astype(BF16)
    parts = []
    for d in range(1, ns):
        to = (s + d) % ns
        at = pl.multiple_of(to * share, share)
        c = remote(wsend.at[pl.ds(at, share)], wrecv.at[d - 1], ws.at[d - 1], wr.at[d - 1], "subband", to)
        c.start()
        parts.append(c)
    total = wsend[pl.ds(pl.multiple_of(s * share, share), share), :].astype(F32)
    for d in range(1, ns):
        parts[d - 1].wait_recv()
        total = total + wrecv[d - 1].astype(F32)
    high = total.astype(BF16)
    low = (total - high.astype(F32)).astype(BF16)
    back = (((1,), (1,)), ((), ()))
    stores = []
    for k in range(ns):
        block = lax.dot_general(high, kern[k], back, preferred_element_type=F32)
        block += lax.dot_general(low, kern[k], back, preferred_element_type=F32)
        dout[k] = block.astype(BF16)
        c = pltpu.make_async_copy(dout.at[k], dirty.at[:, pl.ds(k * depth, depth)], dsem.at[k])
        c.start()
        stores.append(c)

    for c in [near] + cross + passed + parts:
        c.wait_send()

    def drain(i, _):
        @pl.when(z < nf - 1)
        def _():
            right(i).wait_send()

        @pl.when(z > 0)
        def _():
            left(i).wait_send()

        out(i).wait()
        return 0

    lax.fori_loop(0, chunks, drain, 0)
    for c in stores:
        c.wait()


def local(nf, ns, model, kernel, spectrum, observed, subgrid_ids, owners):
    subs, pix = model.shape
    depth, width = kernel.shape
    spans, nblk = subgrid_ids.shape
    chunks = spans * nblk // CHUNK
    share = subs // ns
    dma = pltpu.SemaphoreType.DMA
    vmem = pl.BlockSpec(memory_space=pltpu.VMEM)
    anywhere = pl.BlockSpec(memory_space=pl.ANY)
    flow = pltpu.VMEM((chunks, CHUNK, width), BF16)
    return pl.pallas_call(
        functools.partial(body, nf, ns),
        out_shape=(
            jax.ShapeDtypeStruct((1, spans * nblk, width), BF16),
            jax.ShapeDtypeStruct((share, pix), BF16),
        ),
        in_specs=[anywhere, vmem, vmem, vmem, vmem, pl.BlockSpec(memory_space=pltpu.SMEM)],
        out_specs=(anywhere, anywhere),
        scratch_shapes=[
            pltpu.VMEM((ns, subs, depth), BF16),
            pltpu.VMEM((ns, depth, width), BF16),
            pltpu.VMEM((subs, width), F32),
            pltpu.VMEM((subs, width), BF16),
            pltpu.VMEM((chunks, CHUNK, width), F32),
            flow, flow, flow, flow, flow,
            pltpu.VMEM((subs, width), F32),
            pltpu.VMEM((subs, width), BF16),
            pltpu.VMEM((ns - 1, share, width), BF16),
            pltpu.VMEM((ns, share, depth), BF16),
            dma((ns,)),
            dma((ns,)), dma((ns,)),
            dma((chunks,)), dma((chunks,)), dma((chunks,)), dma((chunks,)),
            dma((ns - 1,)), dma((ns - 1,)),
            dma((chunks,)), dma((ns,)),
        ],
        compiler_params=pltpu.CompilerParams(
            collective_id=0, has_side_effects=True, vmem_limit_bytes=40 * 1024 * 1024
        ),
        name="major_cycle",
    )(model, kernel, spectrum, observed, subgrid_ids, owners)


def solution(mesh):
    return jax.shard_map(
        functools.partial(local, mesh.shape["facet"], mesh.shape["subband"]),
        mesh=mesh,
        in_specs=(
            P(("groups", "facet"), None),
            P("subband", None),
            P(("groups", "subband"), None),
            P(("groups", "subband"), "facet", None, None),
            P("groups", None),
            P("groups"),
        ),
        out_specs=(P(("groups", "subband"), None, None), P(("groups", "facet", "subband"), None)),
        check_vma=False,
    )
```

time: 380 us -> 59.7 us (0.16)
  waiting for transfers between devices: 304 us -> 0 us
  Pallas kernels: 0 us -> 50.9 us
  matrix products: 18.3 us -> 0 us
  other arithmetic: 16.5 us -> 0 us
  between operations: 15.5 us -> 0.65 us
  loops' own time: 10.7 us -> 0 us
  blocking collectives: 8.73 us -> 0 us
    psum x8 -> x0, waiting for transfers between devices: 280 us -> none  [the longest x4 154 us: step(): summed = lax.psum(partial_rows, 'facet')]
    pallas_call x0 -> x1, Pallas kernels: none -> 50.9 us  [local(): pl.pallas_call(functools.partial(body, nf, ns), out_shape=(jax.ShapeDtype...]
    reduce_scatter x1 -> x0, waiting for transfers between devices: 23.6 us -> none  [local(): lax.psum_scatter(weighted.astype(jnp.float32).astype(jnp.bfloat16), 'subb...]
    dot_general x10 -> x0, matrix products: 18.3 us -> none  [the longest x4 7.77 us: step(): lax.dot_general(selector, rounded, (((0,), (0,)), ((), ())), preferred_el...]
    another operation x1 -> x0, loops' own time: 10.7 us -> none  [local(): lax.scan(step, start, jnp.arange(span_count, dtype=jnp.int32))]
    all_gather x1 -> x0, blocking collectives: 8.73 us -> none  [local(): full_kernel = lax.all_gather(kernel, 'subband', axis=0, tiled=True)]
    unnamed x4 -> x14, local copies, waits for them, and re-layouts: 0.01 us -> 7.9 us
    dynamic_update_slice x4 -> x0, other arithmetic: 6.66 us -> none  [local(): lax.scan(step, start, jnp.arange(span_count, dtype=jnp.int32))]
  transfers between devices with their start and end apart: 9 -> 0, of which waited for: 9 -> 0; matrix products, arithmetic and copies ran while one was open for 2% -> 0% of each run, Pallas kernels for 0% -> 0%
where the time goes in v1:
time: 59.7 us; the launch traced here: 59.5 us
  Pallas kernels  50.9 us (85%)
  local copies, waits for them, and re-layouts  7.9 us (13%)
  between operations  0.65 us (1%)
    pallas_call x1, Pallas kernels, local(): pl.pallas_call(functools.partial(body, nf, ns), out_shape=(jax.ShapeDtype...  50.9 us
    unnamed x14, local copies, waits for them, and re-layouts  7.9 us

profile of v1, /device:TPU:1, one launch (start us, length us, event | category | flops | bytes accessed | tf_op | source)
XLA Modules:
  0.0 59.5 jit_solution(3224503207026843986)
XLA Ops:
  0.6 0.0 copy-start
  0.6 2.2 %copy-done = bf16[1024,2048]{1,0:T(8,128)(2,1)S(1)} copy-done((bf16[1024,2048]{1,0:T(8,128)(2,1)S(1)}, bf16[1024,2048]{1,0:T(8,128)(2,1)}, u32[]{:S(2)}) %copy-start) | copy-done | bytes 4194328
  2.8 0.0 copy-start.1
  2.8 1.0 %copy-done.1 = bf16[1,4,512,128]{3,2,1,0:T(8,128)(2,1)S(1)} copy-done((bf16[1,4,512,128]{3,2,1,0:T(8,128)(2,1)S(1)}, bf16[1,4,512,128]{3,2,1,0:T(8,128)(2,1)}, u32[]{:S(2)}) %copy-start.1) | copy-done | bytes 524312
  3.9 0.0 copy-start.2
  3.9 0.9 %copy-done.2 = bf16[512,128]{1,0:T(8,128)(2,1)S(1)} copy-done((bf16[512,128]{1,0:T(8,128)(2,1)S(1)}, bf16[512,128]{1,0:T(8,128)(2,1)}, u32[]{:S(2)}) %copy-start.2) | copy-done | bytes 131096
  4.8 0.0 copy-start.3
  4.8 0.7 %copy-done.3 = s32[4,512]{1,0:T(4,128)S(1)} copy-done((s32[4,512]{1,0:T(4,128)S(1)}, s32[4,512]{1,0:T(4,128)}, u32[]{:S(2)}) %copy-start.3) | copy-done | bytes 8216
  5.5 0.0 copy-start.4
  5.5 0.7 %copy-done.4 = f32[1,128]{1,0:T(1,128)S(1)} copy-done((f32[1,128]{1,0:T(1,128)S(1)}, f32[1,128]{1,0:T(1,128)}, u32[]{:S(2)}) %copy-start.4) | copy-done | bytes 536
  6.1 0.0 copy-start.5
  6.1 0.7 %copy-done.5 = s32[4]{0:T(128)S(1)} copy-done((s32[4]{0:T(128)S(1)}, s32[4]{0:T(128)}, u32[]{:S(2)}) %copy-start.5) | copy-done | bytes 40
  6.8 50.9 %major_cycle.1 = (bf16[1,2048,128]{2,1,0:T(8,128)(2,1)S(1)}, bf16[256,2048]{1,0:T(8,128)(2,1)S(1)}) custom-call(bf16[1024,2048]{1,0:T(8,128)(2,1)S(1)} %copy-done, bf16[512,128]{1,0:T(8,128)(2,1)S(1)} %copy-done.2, f32[1,128]{1,0:T(1,128)S(1)} %copy-done.4, bf16[1,4,512,128]{3,2,1,0:T(8,128)(2,1)S(1)} %copy-done.1, s32[4,512]{1,0:T(4,128)S(1)} %copy-done.3, ...), custom_call_target="tpu_custom_call" | custom-call | tf_op jit(solution)/shard_map/major_cycle/pallas_call | solution.py:232
  57.7 0.8 %copy.10 = bf16[1,2048,128]{2,1,0:T(8,128)(2,1)} copy(bf16[1,2048,128]{2,1,0:T(8,128)(2,1)S(1)} %get-tuple-element.4) | data formatting | bytes 1048576
  58.5 1.0 %copy.11 = bf16[256,2048]{1,0:T(8,128)(2,1)} copy(bf16[256,2048]{1,0:T(8,128)(2,1)S(1)} %get-tuple-element.5) | data formatting | bytes 2097152
Async XLA Ops:
  0.6 2.2 %copy-start = (bf16[1024,2048]{1,0:T(8,128)(2,1)S(1)}, bf16[1024,2048]{1,0:T(8,128)(2,1)}, u32[]{:S(2)}) copy-start(bf16[1024,2048]{1,0:T(8,128)(2,1)} %model.1) | copy-start | bytes 12582916
  2.8 1.0 %copy-start.1 = (bf16[1,4,512,128]{3,2,1,0:T(8,128)(2,1)S(1)}, bf16[1,4,512,128]{3,2,1,0:T(8,128)(2,1)}, u32[]{:S(2)}) copy-start(bf16[1,4,512,128]{3,2,1,0:T(8,128)(2,1)} %observed.1) | copy-start | bytes 1572868
  3.9 0.9 %copy-start.2 = (bf16[512,128]{1,0:T(8,128)(2,1)S(1)}, bf16[512,128]{1,0:T(8,128)(2,1)}, u32[]{:S(2)}) copy-start(bf16[512,128]{1,0:T(8,128)(2,1)} %kernel.1) | copy-start | bytes 393220
  4.8 0.7 %copy-start.3 = (s32[4,512]{1,0:T(4,128)S(1)}, s32[4,512]{1,0:T(4,128)}, u32[]{:S(2)}) copy-start(s32[4,512]{1,0:T(4,128)} %ids.1) | copy-start | bytes 24580
  5.5 0.7 %copy-start.4 = (f32[1,128]{1,0:T(1,128)S(1)}, f32[1,128]{1,0:T(1,128)}, u32[]{:S(2)}) copy-start(f32[1,128]{1,0:T(1,128)} %spectrum.1) | copy-start | bytes 1540
  6.1 0.7 %copy-start.5 = (s32[4]{0:T(128)S(1)}, s32[4]{0:T(128)}, u32[]{:S(2)}) copy-start(s32[4]{0:T(128)} %owners.1) | copy-start | bytes 52

commit v2 on v1

--- a/solution.py
+++ b/solution.py
@@ -10,8 +10,8 @@
 MESH = pl.DeviceIdType.MESH
 F32 = jnp.float32
 BF16 = jnp.bfloat16
-CHUNK = 256
-LAG = 1
+CHUNK = 128
+LAG = 5
 
 
 def remote(src, dst, send, recv, axis, target):
@@ -21,9 +21,10 @@
     )
 
 
-def body(nf, ns, model, kernel, spectrum, observed, ids, owners, residual, dirty,
+def body(nf, ns, model, kernel_h, spectrum, observed, ids_h, owners_h, residual, dirty,
+         kernel, ids, owners, spec_v, small,
          model_v, kern, acc, pred, vals, r_in, l_in, r_out, l_out, res, grid, wsend, wrecv, dout,
-         msem, ks, kr, rs, rr, ls, lr, ws, wr, osem, dsem):
+         ids_v, obs_v, obsem, msem, ks, kr, rs, rr, ls, lr, ws, wr, osem, dsem):
     z = lax.axis_index("facet")
     s = lax.axis_index("subband")
     nx = ns // 2
@@ -34,6 +35,16 @@
     chunks = spans * per
     width = kernel.shape[1]
 
+    first = pltpu.make_async_copy(kernel_h, kernel, small.at[0])
+    first.start()
+    others = [
+        pltpu.make_async_copy(ids_h, ids, small.at[1]),
+        pltpu.make_async_copy(owners_h, owners, small.at[2]),
+        pltpu.make_async_copy(spectrum, spec_v, small.at[3]),
+    ]
+    for c in others:
+        c.start()
+
     order = [s, mate]
     for d in range(1, nx):
         order += [(s + ns - 2 * d) % ns, (mate + ns - 2 * d) % ns]
@@ -43,6 +54,8 @@
         loads.append(pltpu.make_async_copy(model.at[:, pl.ds(at, depth)], model_v.at[n], msem.at[n]))
         loads[-1].start()
 
+    seen_load = pltpu.make_async_copy(observed.at[0], obs_v, obsem)
+    seen_load.start()
     barrier = pltpu.get_barrier_semaphore()
     for d in range(1, ns):
         pl.semaphore_signal(barrier, inc=1, device_id={"subband": (s + d) % ns}, device_id_type=MESH)
@@ -59,6 +72,7 @@
     has_right = jnp.where(z < nf - 1, 1, 0)
     pl.semaphore_wait(barrier, ns - 1 + has_left + has_right)
 
+    first.wait()
     cross = []
     for d in range(1, nx):
         c = remote(kernel, kern.at[s], ks.at[d], kr.at[d], "subband", (s + 2 * d) % ns)
@@ -89,7 +103,11 @@
         add(2 * d + 1, (mate + ns - 2 * d) % ns)
     pred[...] = acc[...].astype(BF16)
 
-    spec = spectrum[...]
+    for c in others + [seen_load]:
+        c.wait()
+    spec = spec_v[...]
+    for c in range(chunks):
+        ids_v[c] = ids[c // per:c // per + 1, c % per * CHUNK:(c % per + 1) * CHUNK]
     offset = z * subs
     grid[...] = jnp.zeros_like(grid)
 
@@ -107,7 +125,7 @@
         @pl.when(t < chunks)
         def _():
             span = t // per
-            row = ids[pl.ds(span, 1), pl.ds(pl.multiple_of((t % per) * CHUNK, CHUNK), CHUNK)] - offset
+            row = ids_v[t] - offset
             column = jnp.broadcast_to(row, (128, CHUNK)).T
             lanes = lax.broadcasted_iota(jnp.int32, (CHUNK, 128), 1)
             pick = jnp.concatenate(
@@ -115,7 +133,7 @@
             )
             rows = jnp.dot(pick, pred[...], preferred_element_type=F32)
             mine = jnp.where(owners[span] == z, 1.0, 0.0).astype(F32)
-            seen = observed[0, span, pl.ds(pl.multiple_of((t % per) * CHUNK, CHUNK), CHUNK), :]
+            seen = obs_v[span, pl.ds(pl.multiple_of((t % per) * CHUNK, CHUNK), CHUNK), :]
             vals[t] = seen.astype(F32) * mine - rows * spec
 
         i = t - LAG * z
@@ -166,7 +184,7 @@
                 res[e] = (vals[e] + (r_in[e].astype(F32) + l_in[e].astype(F32))).astype(BF16)
 
             out(e).start()
-            row = ids[pl.ds(e // per, 1), pl.ds(pl.multiple_of((e % per) * CHUNK, CHUNK), CHUNK)] - offset
+            row = ids_v[e] - offset
             place = (lax.broadcasted_iota(jnp.int32, (subs, CHUNK), 0) == row).astype(F32).astype(BF16)
             grid[...] += jnp.dot(place, res[e], preferred_element_type=F32)
 
@@ -226,7 +244,6 @@
     chunks = spans * nblk // CHUNK
     share = subs // ns
     dma = pltpu.SemaphoreType.DMA
-    vmem = pl.BlockSpec(memory_space=pltpu.VMEM)
     anywhere = pl.BlockSpec(memory_space=pl.ANY)
     flow = pltpu.VMEM((chunks, CHUNK, width), BF16)
     return pl.pallas_call(
@@ -235,9 +252,14 @@
             jax.ShapeDtypeStruct((1, spans * nblk, width), BF16),
             jax.ShapeDtypeStruct((share, pix), BF16),
         ),
-        in_specs=[anywhere, vmem, vmem, vmem, vmem, pl.BlockSpec(memory_space=pltpu.SMEM)],
+        in_specs=[anywhere] * 6,
         out_specs=(anywhere, anywhere),
         scratch_shapes=[
+            pltpu.VMEM((depth, width), BF16),
+            pltpu.VMEM((spans, nblk), jnp.int32),
+            pltpu.SMEM(owners.shape, jnp.int32),
+            pltpu.VMEM((1, width), F32),
+            dma((4,)),
             pltpu.VMEM((ns, subs, depth), BF16),
             pltpu.VMEM((ns, depth, width), BF16),
             pltpu.VMEM((subs, width), F32),
@@ -248,6 +270,9 @@
             pltpu.VMEM((subs, width), BF16),
             pltpu.VMEM((ns - 1, share, width), BF16),
             pltpu.VMEM((ns, share, depth), BF16),
+            pltpu.VMEM((chunks, 1, CHUNK), jnp.int32),
+            pltpu.VMEM(observed.shape[1:], BF16),
+            dma,
             dma((ns,)),
             dma((ns,)), dma((ns,)),
             dma((chunks,)), dma((chunks,)), dma((chunks,)), dma((chunks,)),
@@ -255,7 +280,7 @@
             dma((chunks,)), dma((ns,)),
         ],
         compiler_params=pltpu.CompilerParams(
-            collective_id=0, has_side_effects=True, vmem_limit_bytes=40 * 1024 * 1024
+            collective_id=0, has_side_effects=True, vmem_limit_bytes=60 * 1024 * 1024
         ),
         name="major_cycle",
     )(model, kernel, spectrum, observed, subgrid_ids, owners)

time: 59.7 us -> 41.7 us (0.70)
  Pallas kernels: 50.9 us -> 36.7 us
  local copies, waits for them, and re-layouts: 7.9 us -> 4.17 us
    pallas_call x1, Pallas kernels: 50.9 us -> 36.7 us  [local(): pl.pallas_call(functools.partial(body, nf, ns), out_shape=(jax.ShapeDtype...]
    unnamed x14 -> x2, local copies, waits for them, and re-layouts: 7.9 us -> 4.17 us
where the time goes in v2:
time: 41.7 us; the launch traced here: 41.5 us
  Pallas kernels  36.7 us (88%)
  local copies, waits for them, and re-layouts  4.17 us (10%)
  between operations  0.64 us (2%)
    pallas_call x1, Pallas kernels, local(): pl.pallas_call(functools.partial(body, nf, ns), out_shape=(jax.ShapeDtype...  36.7 us
    unnamed x2, local copies, waits for them, and re-layouts  4.17 us

profile of v2, /device:TPU:1, one launch (start us, length us, event | category | flops | bytes accessed | tf_op | source)
XLA Modules:
  0.0 41.5 jit_solution(10064764771678174179)
XLA Ops:
  0.6 36.7 %major_cycle.1 = (bf16[1,2048,128]{2,1,0:T(8,128)(2,1)}, bf16[256,2048]{1,0:T(8,128)(2,1)}) custom-call(bf16[1024,2048]{1,0:T(8,128)(2,1)} %model.1, bf16[512,128]{1,0:T(8,128)(2,1)} %kernel_h.1, f32[1,128]{1,0:T(1,128)} %spectrum.1, bf16[1,4,512,128]{3,2,1,0:T(8,128)(2,1)} %observed.1, s32[4,512]{1,0:T(4,128)} %ids_h.1, s32[4]{0:T(128)} %owners_h.1), custom_call_target="tpu_custom_call" | custom-call | tf_op jit(solution)/shard_map/major_cycle/pallas_call | solution.py:249
  37.3 1.9 %copy.10 = bf16[1,2048,128]{2,1,0:T(8,128)(2,1)} copy(bf16[1,2048,128]{2,1,0:T(8,128)(2,1)} %get-tuple-element.4) | data formatting | bytes 1048576
  39.2 2.3 %copy.11 = bf16[256,2048]{1,0:T(8,128)(2,1)} copy(bf16[256,2048]{1,0:T(8,128)(2,1)} %get-tuple-element.5) | data formatting | bytes 2097152

commit v3 on v2

--- a/solution.py
+++ b/solution.py
@@ -11,7 +11,9 @@
 F32 = jnp.float32
 BF16 = jnp.bfloat16
 CHUNK = 128
+GROUP = 4
 LAG = 5
+EXTRA = 5
 
 
 def remote(src, dst, send, recv, axis, target):
@@ -21,10 +23,10 @@
     )
 
 
-def body(nf, ns, model, kernel_h, spectrum, observed, ids_h, owners_h, residual, dirty,
+def body(nf, ns, model, kernel_h, spectrum, observed, ids_h, owners_h, residual, total_h, kern_h,
          kernel, ids, owners, spec_v, small,
-         model_v, kern, acc, pred, vals, r_in, l_in, r_out, l_out, res, grid, wsend, wrecv, dout,
-         ids_v, obs_v, obsem, msem, ks, kr, rs, rr, ls, lr, ws, wr, osem, dsem):
+         model_v, kern, acc, pred, vals, r_in, l_in, r_out, l_out, done, px, grid, wsend, wrecv, total_v,
+         ids_v, obs_v, obsem, msem, ks, kr, rs, rr, ls, lr, ps, pr, ws, wr, osem, dsem):
     z = lax.axis_index("facet")
     s = lax.axis_index("subband")
     nx = ns // 2
@@ -33,6 +35,9 @@
     spans, nblk = ids.shape
     per = nblk // CHUNK
     chunks = spans * per
+    early = chunks // 2
+    picks = early // ns
+    messages = chunks + picks
     width = kernel.shape[1]
 
     first = pltpu.make_async_copy(kernel_h, kernel, small.at[0])
@@ -87,22 +92,6 @@
         part = jnp.dot(model_v[n], kern[k], preferred_element_type=F32)
         acc[...] = part if n == 0 else acc[...] + part
 
-    add(0, s)
-    near.wait_recv()
-    add(1, mate)
-    passed = []
-    for d in range(1, nx):
-        src = (s + ns - 2 * d) % ns
-        cross[d - 1].wait_recv()
-        c = remote(kern.at[src], kern.at[src], ks.at[nx + d - 1], kr.at[nx + d - 1], "subband", mate)
-        c.start()
-        passed.append(c)
-        add(2 * d, src)
-    for d in range(1, nx):
-        passed[d - 1].wait_recv()
-        add(2 * d + 1, (mate + ns - 2 * d) % ns)
-    pred[...] = acc[...].astype(BF16)
-
     for c in others + [seen_load]:
         c.wait()
     spec = spec_v[...]
@@ -111,33 +100,77 @@
     offset = z * subs
     grid[...] = jnp.zeros_like(grid)
 
+    passed = []
+    stores = []
+
+    def predict_own():
+        add(0, s)
+        near.wait_recv()
+        add(1, mate)
+        for d in range(1, nx):
+            src = (s + ns - 2 * d) % ns
+            cross[d - 1].wait_recv()
+            c = remote(kern.at[src], kern.at[src], ks.at[nx + d - 1], kr.at[nx + d - 1], "subband", mate)
+            c.start()
+            passed.append(c)
+            add(2 * d, src)
+
+    def predict():
+        for d in range(1, nx):
+            passed[d - 1].wait_recv()
+            add(2 * d + 1, (mate + ns - 2 * d) % ns)
+        pred[...] = acc[...].astype(BF16)
+        stores.append(pltpu.make_async_copy(kern, kern_h, dsem.at[0]))
+        stores[0].start()
+
     def right(i):
         return remote(r_out.at[i], r_in.at[i], rs.at[i], rr.at[i], "facet", z + 1)
 
     def left(i):
         return remote(l_out.at[i], l_in.at[i], ls.at[i], lr.at[i], "facet", z - 1)
 
-    def out(i):
-        at = pl.multiple_of(i * CHUNK, CHUNK)
-        return pltpu.make_async_copy(res.at[i], residual.at[0, pl.ds(at, CHUNK)], osem.at[i])
-
-    def step(t, _):
-        @pl.when(t < chunks)
-        def _():
-            span = t // per
-            row = ids_v[t] - offset
-            column = jnp.broadcast_to(row, (128, CHUNK)).T
-            lanes = lax.broadcasted_iota(jnp.int32, (CHUNK, 128), 1)
-            pick = jnp.concatenate(
-                [(column == lanes + 128 * j).astype(F32).astype(BF16) for j in range(subs // 128)], axis=1
-            )
-            rows = jnp.dot(pick, pred[...], preferred_element_type=F32)
-            mine = jnp.where(owners[span] == z, 1.0, 0.0).astype(F32)
-            seen = obs_v[span, pl.ds(pl.multiple_of((t % per) * CHUNK, CHUNK), CHUNK), :]
-            vals[t] = seen.astype(F32) * mine - rows * spec
+    def out(m, c):
+        at = pl.multiple_of(c * CHUNK, CHUNK)
+        return pltpu.make_async_copy(done.at[m], residual.at[0, pl.ds(at, CHUNK)], osem.at[c])
+
+    def swap(d, k):
+        return remote(done.at[early + k], px.at[s * picks + k], ps.at[d - 1, k], pr.at[d - 1, k],
+                      "subband", (s + d) % ns)
+
+    def seen(c):
+        mine = jnp.where(owners[c // per] == z, 1.0, 0.0).astype(F32)
+        at = pl.multiple_of((c % per) * CHUNK, CHUNK)
+        return obs_v[c // per, pl.ds(at, CHUNK), :].astype(F32) * mine
+
+    def picked(c):
+        column = jnp.broadcast_to(ids_v[c] - offset, (128, CHUNK)).T
+        lanes = lax.broadcasted_iota(jnp.int32, (CHUNK, 128), 1)
+        pick = jnp.concatenate(
+            [(column == lanes + 128 * j).astype(F32).astype(BF16) for j in range(subs // 128)], axis=1
+        )
+        return jnp.dot(pick, pred[...], preferred_element_type=F32)
+
+    def step(t, _, first):
+        def now(m):
+            if first:
+                return jnp.logical_and(m >= 0, m < early)
+            return jnp.logical_and(m < messages, m >= jnp.where(t >= early + EXTRA, 0, early))
+
+        if first:
+            @pl.when(t < early)
+            def _():
+                vals[t] = seen(t)
+        else:
+            @pl.when(t < early + picks)
+            def _():
+                vals[t] = picked(s * picks + t - early)
+
+            @pl.when(jnp.logical_and(t >= early + picks, t < messages))
+            def _():
+                vals[t] = seen(t - picks) - picked(t - picks) * spec
 
         i = t - LAG * z
-        @pl.when(jnp.logical_and(i >= 0, i < chunks))
+        @pl.when(now(i))
         def _():
             @pl.when(z == 0)
             def _():
@@ -153,7 +186,7 @@
                 right(i).start()
 
         j = t - LAG * (nf - 1 - z)
-        @pl.when(jnp.logical_and(j >= 0, j < chunks))
+        @pl.when(now(j))
         def _():
             @pl.when(z == nf - 1)
             def _():
@@ -169,28 +202,52 @@
                 left(j).start()
 
         e = t - LAG * jnp.maximum(z, nf - 1 - z)
-        @pl.when(jnp.logical_and(e >= 0, e < chunks))
+        @pl.when(now(e))
         def _():
             @pl.when(z == 0)
             def _():
-                res[e] = l_out[e]
+                done[e] = l_out[e]
 
             @pl.when(z == nf - 1)
             def _():
-                res[e] = r_out[e]
+                done[e] = r_out[e]
 
             @pl.when(jnp.logical_and(z > 0, z < nf - 1))
             def _():
-                res[e] = (vals[e] + (r_in[e].astype(F32) + l_in[e].astype(F32))).astype(BF16)
-
-            out(e).start()
-            row = ids_v[e] - offset
-            place = (lax.broadcasted_iota(jnp.int32, (subs, CHUNK), 0) == row).astype(F32).astype(BF16)
-            grid[...] += jnp.dot(place, res[e], preferred_element_type=F32)
+                done[e] = (vals[e] + (r_in[e].astype(F32) + l_in[e].astype(F32))).astype(BF16)
+
+        if not first:
+            @pl.when(jnp.logical_and(e >= early, e < early + picks))
+            def _():
+                px[s * picks + e - early] = done[e]
+                for d in range(1, ns):
+                    swap(d, e - early).start()
+
+            @pl.when(jnp.logical_and(e >= early + picks, e < messages))
+            def _():
+                out(e, e - picks).start()
+                place = (lax.broadcasted_iota(jnp.int32, (subs, CHUNK), 0) == ids_v[e - picks] - offset)
+                grid[...] += jnp.dot(place.astype(F32).astype(BF16), done[e], preferred_element_type=F32)
 
         return 0
 
-    lax.fori_loop(0, chunks + LAG * (nf - 1), step, 0)
+    lax.fori_loop(0, early, functools.partial(step, first=True), 0)
+    predict_own()
+    lax.fori_loop(early, early + EXTRA, functools.partial(step, first=True), 0)
+    predict()
+    lax.fori_loop(early, messages + LAG * (nf - 1), functools.partial(step, first=False), 0)
+
+    for d in range(1, ns):
+        for k in range(picks):
+            swap(d, k).wait_recv()
+    for c in range(0, early, GROUP):
+        for n in range(c, c + GROUP):
+            done[n] = (done[n].astype(F32) - px[n].astype(F32) * spec).astype(BF16)
+            out(n, n).start()
+        row = jnp.concatenate([ids_v[n] for n in range(c, c + GROUP)], axis=1) - offset
+        place = lax.broadcasted_iota(jnp.int32, (subs, GROUP * CHUNK), 0) == row
+        rows = jnp.concatenate([done[n] for n in range(c, c + GROUP)], axis=0)
+        grid[...] += jnp.dot(place.astype(F32).astype(BF16), rows, preferred_element_type=F32)
 
     share = subs // ns
     wsend[...] = (grid[...] * spec).astype(BF16)
@@ -205,36 +262,63 @@
     for d in range(1, ns):
         parts[d - 1].wait_recv()
         total = total + wrecv[d - 1].astype(F32)
+    total_v[...] = total
+    stores.append(pltpu.make_async_copy(total_v, total_h, dsem.at[1]))
+    stores[1].start()
+
+    for c in [near] + cross + passed + parts:
+        c.wait_send()
+
+    def drain(i, _):
+        @pl.when(z < nf - 1)
+        def _():
+            right(i).wait_send()
+
+        @pl.when(z > 0)
+        def _():
+            left(i).wait_send()
+
+        return 0
+
+    lax.fori_loop(0, messages, drain, 0)
+    for d in range(1, ns):
+        for k in range(picks):
+            swap(d, k).wait_send()
+    for c in range(chunks):
+        out(c if c < early else c + picks, c).wait()
+    for c in stores:
+        c.wait()
+
+
+def finish(residual, total_h, kern_h, res_out, dirty, total_v, kern, dout, res_v, sem, ksem, dsem):
+    ns, depth, _ = kern.shape
+    loads = [pltpu.make_async_copy(kern_h.at[k], kern.at[k], ksem.at[k]) for k in range(ns)]
+    first = pltpu.make_async_copy(total_h, total_v, sem.at[0])
+    inward = pltpu.make_async_copy(residual, res_v, sem.at[1])
+    outward = pltpu.make_async_copy(res_v, res_out, sem.at[2])
+    first.start()
+    for c in loads:
+        c.start()
+    inward.start()
+    first.wait()
+    total = total_v[...]
+    inward.wait()
+    outward.start()
     high = total.astype(BF16)
     low = (total - high.astype(F32)).astype(BF16)
     back = (((1,), (1,)), ((), ()))
     stores = []
     for k in range(ns):
+        loads[k].wait()
         block = lax.dot_general(high, kern[k], back, preferred_element_type=F32)
         block += lax.dot_general(low, kern[k], back, preferred_element_type=F32)
         dout[k] = block.astype(BF16)
         c = pltpu.make_async_copy(dout.at[k], dirty.at[:, pl.ds(k * depth, depth)], dsem.at[k])
         c.start()
         stores.append(c)
-
-    for c in [near] + cross + passed + parts:
-        c.wait_send()
-
-    def drain(i, _):
-        @pl.when(z < nf - 1)
-        def _():
-            right(i).wait_send()
-
-        @pl.when(z > 0)
-        def _():
-            left(i).wait_send()
-
-        out(i).wait()
-        return 0
-
-    lax.fori_loop(0, chunks, drain, 0)
     for c in stores:
         c.wait()
+    outward.wait()
 
 
 def local(nf, ns, model, kernel, spectrum, observed, subgrid_ids, owners):
@@ -245,15 +329,19 @@
     share = subs // ns
     dma = pltpu.SemaphoreType.DMA
     anywhere = pl.BlockSpec(memory_space=pl.ANY)
-    flow = pltpu.VMEM((chunks, CHUNK, width), BF16)
-    return pl.pallas_call(
+    early = chunks // 2
+    picks = early // ns
+    messages = chunks + picks
+    flow = pltpu.VMEM((messages, CHUNK, width), BF16)
+    residual, total, kern = pl.pallas_call(
         functools.partial(body, nf, ns),
         out_shape=(
             jax.ShapeDtypeStruct((1, spans * nblk, width), BF16),
-            jax.ShapeDtypeStruct((share, pix), BF16),
+            jax.ShapeDtypeStruct((share, width), F32),
+            jax.ShapeDtypeStruct((ns, depth, width), BF16),
         ),
         in_specs=[anywhere] * 6,
-        out_specs=(anywhere, anywhere),
+        out_specs=(anywhere,) * 3,
         scratch_shapes=[
             pltpu.VMEM((depth, width), BF16),
             pltpu.VMEM((spans, nblk), jnp.int32),
@@ -264,26 +352,45 @@
             pltpu.VMEM((ns, depth, width), BF16),
             pltpu.VMEM((subs, width), F32),
             pltpu.VMEM((subs, width), BF16),
-            pltpu.VMEM((chunks, CHUNK, width), F32),
+            pltpu.VMEM((messages, CHUNK, width), F32),
             flow, flow, flow, flow, flow,
+            pltpu.VMEM((early, CHUNK, width), BF16),
             pltpu.VMEM((subs, width), F32),
             pltpu.VMEM((subs, width), BF16),
             pltpu.VMEM((ns - 1, share, width), BF16),
-            pltpu.VMEM((ns, share, depth), BF16),
+            pltpu.VMEM((share, width), F32),
             pltpu.VMEM((chunks, 1, CHUNK), jnp.int32),
             pltpu.VMEM(observed.shape[1:], BF16),
             dma,
             dma((ns,)),
             dma((ns,)), dma((ns,)),
-            dma((chunks,)), dma((chunks,)), dma((chunks,)), dma((chunks,)),
+            dma((messages,)), dma((messages,)), dma((messages,)), dma((messages,)),
+            dma((ns - 1, picks)), dma((ns - 1, picks)),
             dma((ns - 1,)), dma((ns - 1,)),
-            dma((chunks,)), dma((ns,)),
+            dma((chunks,)), dma((2,)),
         ],
         compiler_params=pltpu.CompilerParams(
             collective_id=0, has_side_effects=True, vmem_limit_bytes=60 * 1024 * 1024
         ),
         name="major_cycle",
     )(model, kernel, spectrum, observed, subgrid_ids, owners)
+    return pl.pallas_call(
+        finish,
+        out_shape=(
+            jax.ShapeDtypeStruct(residual.shape, BF16),
+            jax.ShapeDtypeStruct((share, pix), BF16),
+        ),
+        in_specs=[anywhere] * 3,
+        out_specs=(anywhere,) * 2,
+        scratch_shapes=[
+            pltpu.VMEM(total.shape, F32), pltpu.VMEM(kern.shape, BF16),
+            pltpu.VMEM((ns, share, depth), BF16),
+            pltpu.VMEM(residual.shape, BF16),
+            dma((3,)), dma((ns,)), dma((ns,)),
+        ],
+        compiler_params=pltpu.CompilerParams(vmem_limit_bytes=60 * 1024 * 1024),
+        name="back",
+    )(residual, total, kern)
 
 
 def solution(mesh):

time: 41.7 us -> 38 us (0.911)
  local copies, waits for them, and re-layouts: 4.17 us -> 0 us
  Pallas kernels: 36.7 us -> 37.2 us
    unnamed x2 -> x0, local copies, waits for them, and re-layouts: 4.17 us -> none
    pallas_call x0 -> x1, Pallas kernels: none -> 3.36 us  [local(): pl.pallas_call(finish, out_shape=(jax.ShapeDtypeStruct(residual.shape, BF...]
    pallas_call x1, Pallas kernels: 36.7 us -> 33.8 us  [local(): pl.pallas_call(functools.partial(body, nf, ns), out_shape=(jax.ShapeDtype...]
where the time goes in v3:
time: 38 us; the launch traced here: 37.8 us
  Pallas kernels  37.2 us (98%)
  between operations  0.64 us (2%)
    pallas_call x1, Pallas kernels, local(): pl.pallas_call(functools.partial(body, nf, ns), out_shape=(jax.ShapeDtype...  33.8 us
    pallas_call x1, Pallas kernels, local(): pl.pallas_call(finish, out_shape=(jax.ShapeDtypeStruct(residual.shape, BF...  3.36 us

profile of v3, /device:TPU:1, one launch (start us, length us, event | category | flops | bytes accessed | tf_op | source)
XLA Modules:
  0.0 37.8 jit_solution(14193931247372131992)
XLA Ops:
  0.6 33.8 %major_cycle.1 = (bf16[1,2048,128]{2,1,0:T(8,128)(2,1)}, f32[256,128]{1,0:T(8,128)}, bf16[4,512,128]{2,1,0:T(8,128)(2,1)}) custom-call(bf16[1024,2048]{1,0:T(8,128)(2,1)} %model.1, bf16[512,128]{1,0:T(8,128)(2,1)} %kernel_h.1, f32[1,128]{1,0:T(1,128)} %spectrum.1, bf16[1,4,512,128]{3,2,1,0:T(8,128)(2,1)} %observed.1, s32[4,512]{1,0:T(4,128)} %ids_h.1, s32[4]{0:T(128)} %owners_h.1), custom_call_target="tpu_custom_call" | custom-call | tf_op jit(solution)/shard_map/major_cycle/pallas_call | solution.py:336
  34.5 3.4 %back.1 = (bf16[1,2048,128]{2,1,0:T(8,128)(2,1)}, bf16[256,2048]{1,0:T(8,128)(2,1)}) custom-call(bf16[1,2048,128]{2,1,0:T(8,128)(2,1)} %get-tuple-element.5.residual, f32[256,128]{1,0:T(8,128)} %get-tuple-element.6.total_h, bf16[4,512,128]{2,1,0:T(8,128)(2,1)} %get-tuple-element.7.kern_h), custom_call_target="tpu_custom_call" | custom-call | tf_op jit(solution)/shard_map/back/pallas_call | solution.py:377

commit v4 on v3

--- a/solution.py
+++ b/solution.py
@@ -78,13 +78,22 @@
     pl.semaphore_wait(barrier, ns - 1 + has_left + has_right)
 
     first.wait()
-    cross = []
+    half = depth // 2
+    cross, direct = [], []
     for d in range(1, nx):
-        c = remote(kernel, kern.at[s], ks.at[d], kr.at[d], "subband", (s + 2 * d) % ns)
+        c = remote(kernel.at[pl.ds(0, half)], kern.at[s, pl.ds(0, half)], ks.at[d], kr.at[d],
+                   "subband", (s + 2 * d) % ns)
         c.start()
         cross.append(c)
     near = remote(kernel, kern.at[s], ks.at[0], kr.at[0], "subband", mate)
     near.start()
+    for d in range(1, nx):
+        for q, peer in enumerate((s, mate)):
+            n = ns + 2 * (d - 1) + q
+            c = remote(kernel.at[pl.ds(half, half)], kern.at[s, pl.ds(half, half)], ks.at[n], kr.at[n],
+                       "subband", (peer + 2 * d) % ns)
+            c.start()
+            direct.append(c)
     kern[s] = kernel[...]
 
     def add(n, k):
@@ -110,14 +119,17 @@
         for d in range(1, nx):
             src = (s + ns - 2 * d) % ns
             cross[d - 1].wait_recv()
-            c = remote(kern.at[src], kern.at[src], ks.at[nx + d - 1], kr.at[nx + d - 1], "subband", mate)
+            c = remote(kern.at[src, pl.ds(0, half)], kern.at[src, pl.ds(0, half)], ks.at[nx + d - 1],
+                       kr.at[nx + d - 1], "subband", mate)
             c.start()
             passed.append(c)
-            add(2 * d, src)
 
     def predict():
         for d in range(1, nx):
+            direct[2 * d - 2].wait_recv()
+            add(2 * d, (s + ns - 2 * d) % ns)
             passed[d - 1].wait_recv()
+            direct[2 * d - 1].wait_recv()
             add(2 * d + 1, (mate + ns - 2 * d) % ns)
         pred[...] = acc[...].astype(BF16)
         stores.append(pltpu.make_async_copy(kern, kern_h, dsem.at[0]))
@@ -266,7 +278,7 @@
     stores.append(pltpu.make_async_copy(total_v, total_h, dsem.at[1]))
     stores[1].start()
 
-    for c in [near] + cross + passed + parts:
+    for c in [near] + cross + direct + passed + parts:
         c.wait_send()
 
     def drain(i, _):
@@ -363,7 +375,7 @@
             pltpu.VMEM(observed.shape[1:], BF16),
             dma,
             dma((ns,)),
-            dma((ns,)), dma((ns,)),
+            dma((2 * ns,)), dma((2 * ns,)),
             dma((messages,)), dma((messages,)), dma((messages,)), dma((messages,)),
             dma((ns - 1, picks)), dma((ns - 1, picks)),
             dma((ns - 1,)), dma((ns - 1,)),

time: 38 us -> 38.8 us (1.021)
  Pallas kernels: 37.2 us -> 38 us
    pallas_call x1, Pallas kernels: 33.8 us -> 34.6 us  [local(): pl.pallas_call(functools.partial(body, nf, ns), out_shape=(jax.ShapeDtype...]
where the time goes in v4:
time: 38.8 us; the launch traced here: 38.6 us
  Pallas kernels  38 us (98%)
  between operations  0.64 us (2%)
    pallas_call x1, Pallas kernels, local(): pl.pallas_call(functools.partial(body, nf, ns), out_shape=(jax.ShapeDtype...  34.6 us
    pallas_call x1, Pallas kernels, local(): pl.pallas_call(finish, out_shape=(jax.ShapeDtypeStruct(residual.shape, BF...  3.36 us

profile of v4, /device:TPU:1, one launch (start us, length us, event | category | flops | bytes accessed | tf_op | source)
XLA Modules:
  0.0 38.6 jit_solution(12540019333271261146)
XLA Ops:
  0.6 34.6 %major_cycle.1 = (bf16[1,2048,128]{2,1,0:T(8,128)(2,1)}, f32[256,128]{1,0:T(8,128)}, bf16[4,512,128]{2,1,0:T(8,128)(2,1)}) custom-call(bf16[1024,2048]{1,0:T(8,128)(2,1)} %model.1, bf16[512,128]{1,0:T(8,128)(2,1)} %kernel_h.1, f32[1,128]{1,0:T(1,128)} %spectrum.1, bf16[1,4,512,128]{3,2,1,0:T(8,128)(2,1)} %observed.1, s32[4,512]{1,0:T(4,128)} %ids_h.1, s32[4]{0:T(128)} %owners_h.1), custom_call_target="tpu_custom_call" | custom-call | tf_op jit(solution)/shard_map/major_cycle/pallas_call | solution.py:348
  35.2 3.4 %back.1 = (bf16[1,2048,128]{2,1,0:T(8,128)(2,1)}, bf16[256,2048]{1,0:T(8,128)(2,1)}) custom-call(bf16[1,2048,128]{2,1,0:T(8,128)(2,1)} %get-tuple-element.5.residual, f32[256,128]{1,0:T(8,128)} %get-tuple-element.6.total_h, bf16[4,512,128]{2,1,0:T(8,128)(2,1)} %get-tuple-element.7.kern_h), custom_call_target="tpu_custom_call" | custom-call | tf_op jit(solution)/shard_map/back/pallas_call | solution.py:389

commit v5 on v3

--- a/solution.py
+++ b/solution.py
@@ -11,7 +11,7 @@
 F32 = jnp.float32
 BF16 = jnp.bfloat16
 CHUNK = 128
-GROUP = 4
+GROUP = 8
 LAG = 5
 EXTRA = 5
 
@@ -258,6 +258,27 @@
         c = remote(wsend.at[pl.ds(at, share)], wrecv.at[d - 1], ws.at[d - 1], wr.at[d - 1], "subband", to)
         c.start()
         parts.append(c)
+    for c in [near] + cross + passed:
+        c.wait_send()
+
+    def drain(i, _):
+        @pl.when(z < nf - 1)
+        def _():
+            right(i).wait_send()
+
+        @pl.when(z > 0)
+        def _():
+            left(i).wait_send()
+
+        return 0
+
+    lax.fori_loop(0, messages, drain, 0)
+    for d in range(1, ns):
+        for k in range(picks):
+            swap(d, k).wait_send()
+    for c in range(chunks):
+        out(c if c < early else c + picks, c).wait()
+
     total = wsend[pl.ds(pl.multiple_of(s * share, share), share), :].astype(F32)
     for d in range(1, ns):
         parts[d - 1].wait_recv()
@@ -266,26 +287,8 @@
     stores.append(pltpu.make_async_copy(total_v, total_h, dsem.at[1]))
     stores[1].start()
 
-    for c in [near] + cross + passed + parts:
+    for c in parts:
         c.wait_send()
-
-    def drain(i, _):
-        @pl.when(z < nf - 1)
-        def _():
-            right(i).wait_send()
-
-        @pl.when(z > 0)
-        def _():
-            left(i).wait_send()
-
-        return 0
-
-    lax.fori_loop(0, messages, drain, 0)
-    for d in range(1, ns):
-        for k in range(picks):
-            swap(d, k).wait_send()
-    for c in range(chunks):
-        out(c if c < early else c + picks, c).wait()
     for c in stores:
         c.wait()
 

time: 38 us -> 38 us (level)
  no operation moved by 1% of the time
where the time goes in v5:
time: 38 us; the launch traced here: 37.8 us
  Pallas kernels  37.2 us (98%)
  between operations  0.64 us (2%)
    pallas_call x1, Pallas kernels, local(): pl.pallas_call(functools.partial(body, nf, ns), out_shape=(jax.ShapeDtype...  33.8 us
    pallas_call x1, Pallas kernels, local(): pl.pallas_call(finish, out_shape=(jax.ShapeDtypeStruct(residual.shape, BF...  3.36 us

profile of v5, /device:TPU:1, one launch (start us, length us, event | category | flops | bytes accessed | tf_op | source)
XLA Modules:
  0.0 37.8 jit_solution(3304032111130424522)
XLA Ops:
  0.6 33.8 %major_cycle.1 = (bf16[1,2048,128]{2,1,0:T(8,128)(2,1)}, f32[256,128]{1,0:T(8,128)}, bf16[4,512,128]{2,1,0:T(8,128)(2,1)}) custom-call(bf16[1024,2048]{1,0:T(8,128)(2,1)} %model.1, bf16[512,128]{1,0:T(8,128)(2,1)} %kernel_h.1, f32[1,128]{1,0:T(1,128)} %spectrum.1, bf16[1,4,512,128]{3,2,1,0:T(8,128)(2,1)} %observed.1, s32[4,512]{1,0:T(4,128)} %ids_h.1, s32[4]{0:T(128)} %owners_h.1), custom_call_target="tpu_custom_call" | custom-call | tf_op jit(solution)/shard_map/major_cycle/pallas_call | solution.py:339
  34.5 3.4 %back.1 = (bf16[1,2048,128]{2,1,0:T(8,128)(2,1)}, bf16[256,2048]{1,0:T(8,128)(2,1)}) custom-call(bf16[1,2048,128]{2,1,0:T(8,128)(2,1)} %get-tuple-element.5.residual, f32[256,128]{1,0:T(8,128)} %get-tuple-element.6.total_h, bf16[4,512,128]{2,1,0:T(8,128)(2,1)} %get-tuple-element.7.kern_h), custom_call_target="tpu_custom_call" | custom-call | tf_op jit(solution)/shard_map/back/pallas_call | solution.py:380
